TPU v7x, 512 devices: a whole 4x4x16 slice. The times are simulated.
512 devices in a mesh: seq: 128 (over z, x, core), dp: 4 (over y).
Axes of the slice: x: 4, y: 4, z: 16, core: 2. Of those that a mesh axis runs over, the one named last changes fastest.
Arguments:
- queries: bfloat16 [4, 32768, 512], P('dp', 'seq'), may hold values from -1.75 to 1.75
- keys: bfloat16 [4, 32768, 512], P('dp', 'seq'), may hold values from -1.75 to 1.75
- values: bfloat16 [4, 32768, 512], P('dp', 'seq'), may hold values from -6 to 6
- gates: bfloat16 [4, 32768, 512], P('dp', 'seq'), may hold values from -24 to 24
- out_weight: bfloat16 [512, 1024], replicated, may hold values from -0.25 to 0.25
- out_grad: bfloat16 [4, 32768, 1024], P('dp', 'seq'), may hold values from -6 to 6
- lengths: int32 [4, 4], P('dp'), may hold values from 1 to 16384, 32768 in all within a row
- pattern: int32 [4, 128, 2], P('dp', 'seq'), may hold values 0 or 1
Outputs:
- query_grad: bfloat16 [4, 32768, 512], P('dp', 'seq')
- key_grad: bfloat16 [4, 32768, 512], P('dp', 'seq')
- value_grad: bfloat16 [4, 32768, 512], P('dp', 'seq')
- gate_grad: bfloat16 [4, 32768, 512], P('dp', 'seq')
- weight_grad: float32 [512, 1024], P('seq')
Inputs may be any that keep to these rules, and one draw needn't show every extreme that they name: Each row of lengths sums to 32768, and its largest entry is exactly 16384.
All inputs are finite; a program needn't handle non-finite values. No bound on the sum of `pattern` on one device may be relied on, other than what follows from the above.
Results may differ from a plain program's by a relative error of at most 0.0065.
Values may be sent and summed in bfloat16 or wider, within the bound.
A program may use at most 64 MiB of HBM per device.

v0:
```python
import jax
import jax.numpy as jnp
from jax import lax
from jax.sharding import PartitionSpec as P

HEAD_DIM = 128


EPS = 1e-05


def shifted(array, axis, by):
    peers = lax.axis_size(axis)
    pairs = [(i, i + by) for i in range(peers) if 0 <= i + by < peers]
    return lax.ppermute(array, axis, pairs)


def silu_slope(scores):
    sigma = jax.nn.sigmoid(scores)
    return sigma * (1.0 + scores * (1.0 - sigma))


def visible(query_block, pattern_row, doc_ends, block_rows):
    offsets = jnp.arange(block_rows, dtype=jnp.int32)
    query_pos = query_block * block_rows + offsets
    key_block = query_block - jnp.arange(pattern_row.shape[0] + 1, dtype=jnp.int32)
    key_pos = (key_block[:, None] * block_rows + offsets[None, :]).reshape(-1)
    allowed = jnp.concatenate([jnp.ones((1,), jnp.float32), (pattern_row > 0).astype(jnp.float32)])
    allowed_keys = jnp.repeat(allowed, block_rows)
    query_doc = jnp.sum((query_pos[:, None] >= doc_ends[None, :]).astype(jnp.int32), axis=1)
    key_doc = jnp.sum((key_pos[:, None] >= doc_ends[None, :]).astype(jnp.int32), axis=1)
    keep = (
        (query_doc[:, None] == key_doc[None, :])
        & (key_pos[None, :] <= query_pos[:, None])
        & (key_pos[None, :] >= 0)
    )
    return keep.astype(jnp.float32) * allowed_keys[None, :]


def local(queries, keys, values, gates, out_weight, out_grad, lengths, pattern):
    block_rows = queries.shape[1]
    width = queries.shape[2]
    heads = width // HEAD_DIM
    band = pattern.shape[2]
    scale = 1.0 / ((band + 1) * block_rows)
    position = lax.axis_index("seq")
    doc_ends = jnp.cumsum(lengths[0])
    own_query = queries[0]
    own_key = keys[0]
    own_value = values[0]
    gate_rows = gates[0]
    grad_rows = out_grad[0]
    pattern_row = pattern[0, 0]
    key_list = [own_key]
    value_list = [own_value]
    for offset in range(1, band + 1):
        moved_key, moved_value = shifted((own_key, own_value), "seq", offset)
        key_list.append(moved_key)
        value_list.append(moved_value)
    key_band = jnp.concatenate(key_list, axis=0).reshape(-1, heads, HEAD_DIM)
    value_band = jnp.concatenate(value_list, axis=0).reshape(-1, heads, HEAD_DIM)
    query_heads = own_query.reshape(block_rows, heads, HEAD_DIM)
    visible_mask = visible(position, pattern_row, doc_ends, block_rows)
    scores = jnp.einsum("qhd,khd->hqk", query_heads, key_band, preferred_element_type=jnp.float32)
    weights = (jax.nn.silu(scores) * visible_mask[None] * scale).astype(jnp.bfloat16)
    mixed = jnp.einsum(
        "hqk,khd->qhd", weights, value_band, preferred_element_type=jnp.float32
    ).reshape(block_rows, width)
    centre = jnp.mean(mixed, axis=1, keepdims=True)
    spread = jnp.mean((mixed - centre) ** 2, axis=1, keepdims=True)
    inv_root = lax.rsqrt(spread + EPS)
    normed = (mixed - centre) * inv_root
    gated = (normed * gate_rows).astype(jnp.bfloat16)
    gated_grad = jnp.einsum("rd,fd->rf", grad_rows, out_weight, preferred_element_type=jnp.float32)
    gate_grad = (gated_grad * normed).astype(jnp.bfloat16)
    normed_grad = gated_grad * gate_rows
    mixed_grad = inv_root * (
        normed_grad
        - jnp.mean(normed_grad, axis=1, keepdims=True)
        - normed * jnp.mean(normed_grad * normed, axis=1, keepdims=True)
    )
    mixed_grad = mixed_grad.astype(jnp.bfloat16)
    grad_heads = mixed_grad.reshape(block_rows, heads, HEAD_DIM)
    weight_slope = jnp.einsum(
        "qhd,khd->hqk", grad_heads, value_band, preferred_element_type=jnp.float32
    )
    score_grad = (weight_slope * visible_mask[None] * scale * silu_slope(scores)).astype(
        jnp.bfloat16
    )
    query_grad = jnp.einsum(
        "hqk,khd->qhd", score_grad, key_band, preferred_element_type=jnp.float32
    )
    query_grad = query_grad.reshape(block_rows, width).astype(jnp.bfloat16)
    key_terms = jnp.einsum(
        "hqk,qhd->khd", score_grad, query_heads, preferred_element_type=jnp.float32
    )
    value_terms = jnp.einsum(
        "hqk,qhd->khd", weights, grad_heads, preferred_element_type=jnp.float32
    )
    key_terms = key_terms.reshape(band + 1, block_rows, width).astype(jnp.bfloat16)
    value_terms = value_terms.reshape(band + 1, block_rows, width).astype(jnp.bfloat16)
    key_total = lax.optimization_barrier(key_terms[0]).astype(jnp.float32)
    value_total = lax.optimization_barrier(value_terms[0]).astype(jnp.float32)
    for offset in range(1, band + 1):
        back_key, back_value = shifted((key_terms[offset], value_terms[offset]), "seq", -offset)
        key_total = key_total + back_key.astype(jnp.float32)
        value_total = value_total + back_value.astype(jnp.float32)
    share = width // lax.axis_size("seq")
    local_term = jnp.einsum("rf,rd->fd", gated, grad_rows, preferred_element_type=jnp.float32)
    summed = lax.psum(local_term, ("seq", "dp"))
    weight_part = lax.dynamic_slice_in_dim(summed, position * share, share, 0)
    return (
        query_grad[None],
        key_total.astype(jnp.bfloat16)[None],
        value_total.astype(jnp.bfloat16)[None],
        gate_grad[None],
        weight_part,
    )


def solution(mesh):
    return jax.shard_map(
        local,
        mesh=mesh,
        in_specs=(
            P("dp", "seq", None),
            P("dp", "seq", None),
            P("dp", "seq", None),
            P("dp", "seq", None),
            P(),
            P("dp", "seq", None),
            P("dp", None),
            P("dp", "seq", None),
        ),
        out_specs=(
            P("dp", "seq", None),
            P("dp", "seq", None),
            P("dp", "seq", None),
            P("dp", "seq", None),
            P("seq", None),
        ),
        check_vma=False,
    )
```

profile of v0, /device:TPU:1, one launch (start us, length us, event | category | flops | bytes accessed | tf_op | source)
XLA Modules:
  0.0 537.0 jit_solution(5002235556178650659)
XLA Ops:
  7.2 1.2 copy.64
  8.4 4.7 collective-permute-start.1
  13.1 3.2 collective-permute-start
  16.4 3.6 collective-permute-start.3
  19.9 1.9 collective-permute-start.2
  23.7 1.1 copy.69
  25.4 1.5 and_select_fusion
  26.9 1.1 copy.68
  28.1 1.2 copy.67
  29.3 4.4 fusion.5
  33.7 1.1 copy.71
  35.0 1.9 fusion.28
  38.7 0.9 fusion.20
  39.8 2.2 fusion.11
  42.0 3.4 fusion.9
  45.4 1.2 copy-done.3
  47.6 1.8 fusion.12
  52.0 1.8 copy.89
  53.8 1.8 copy.88
  55.6 1.8 copy.83
  57.4 2.8 collective-permute-start.4
  60.3 1.9 collective-permute-start.6
  62.2 1.3 collective-permute-start.7
  63.5 1.3 collective-permute-start.5
  64.8 2.2 convolution_convert_fusion.2
  67.0 1.8 copy.91
  69.9 3.2 collective-permute-done.7
  73.1 1.8 fusion.19
  74.9 4.0 collective-permute-done.5
  79.0 1.8 fusion.18
  80.8 448.0 %all-reduce.2.cloned.1.call-done = f32[512,1024]{1,0:T(8,128)} async-done(((f32[512,1024]{1,0:T(8,128)}), f32[512,1024]{1,0:T(8,128)}) %all-reduce.2.cloned.1.call-update) | async-done | bytes 2097168 | tf_op jit(solution)/shard_map/psum | solution.py:110
  528.8 1.4 constant_dynamic-slice_fusion
  (81 shorter events, 9.1 us)
Async XLA Ops:
  7.2 30.9 %copy-start = (bf16[512,1024]{1,0:T(8,128)(2,1)S(1)}, bf16[512,1024]{1,0:T(8,128)(2,1)}, u32[]{:S(2)}) copy-start(bf16[512,1024]{1,0:T(8,128)(2,1)} %param.12) | copy-start | bytes 3145732
  7.2 17.9 %copy-start.11 = (bf16[1,256,512]{2,1,0:T(8,128)(2,1)S(1)}, bf16[1,256,512]{2,1,0:T(8,128)(2,1)}, u32[]{:S(2)}) copy-start(bf16[1,256,512]{2,1,0:T(8,128)(2,1)} %param.8) | copy-start | bytes 786436
  7.2 18.0 %copy-start.1 = (bf16[1,256,512]{2,1,0:T(8,128)(2,1)S(1)}, bf16[1,256,512]{2,1,0:T(8,128)(2,1)}, u32[]{:S(2)}) copy-start(bf16[1,256,512]{2,1,0:T(8,128)(2,1)} %param.11) | copy-start | bytes 786436
  7.2 521.6 %all-reduce.2.cloned.1.call-start = ((), (), s32[]{:S(2)}) async-start(), calls=%async_computation | async-start | bytes 4194304 | tf_op jit(solution)/shard_map/psum | solution.py:110
  8.4 18.5 %collective-permute-start.1 = (bf16[256,512]{0,1:T(8,128)(2,1)S(1)}, bf16[256,512]{0,1:T(8,128)(2,1)}, u32[]{:S(2)}, u32[]{:S(2)}) collective-permute-start(bf16[256,512]{0,1:T(8,128)(2,1)S(1)} %bitcast.102), channel_id=1, source_target_pairs={{0,8},{4,12},{8,16},{12,20},{16,24},{20,28},{24,32},{28,36},{32,40... | collective-permute-start | bytes 786440 | tf_op jit(solution)/shard_map/ppermute | solution.py:15
  13.1 14.9 %collective-permute-start = (bf16[256,512]{0,1:T(8,128)(2,1)S(1)}, bf16[256,512]{0,1:T(8,128)(2,1)}, u32[]{:S(2)}, u32[]{:S(2)}) collective-permute-start(bf16[256,512]{0,1:T(8,128)(2,1)S(1)} %bitcast.103), channel_id=1, source_target_pairs={{0,4},{4,8},{8,12},{12,16},{16,20},{20,24},{24,28},{28,32},{32,36}... | collective-permute-start | bytes 786440 | tf_op jit(solution)/shard_map/ppermute | solution.py:15
  16.4 17.4 %collective-permute-start.3 = (bf16[256,512]{1,0:T(8,128)(2,1)}, bf16[256,512]{1,0:T(8,128)(2,1)}, u32[]{:S(2)}, u32[]{:S(2)}) collective-permute-start(bf16[256,512]{1,0:T(8,128)(2,1)} %bitcast.112), channel_id=1, source_target_pairs={{0,8},{4,12},{8,16},{12,20},{16,24},{20,28},{24,32},{28,36},{32,40... | collective-permute-start | bytes 786440 | tf_op jit(solution)/shard_map/ppermute | solution.py:15
  19.9 14.9 %collective-permute-start.2 = (bf16[256,512]{1,0:T(8,128)(2,1)}, bf16[256,512]{1,0:T(8,128)(2,1)S(1)}, u32[]{:S(2)}, u32[]{:S(2)}) collective-permute-start(bf16[256,512]{1,0:T(8,128)(2,1)} %bitcast.113), channel_id=1, source_target_pairs={{0,4},{4,8},{8,12},{12,16},{16,20},{20,24},{24,28},{28,32},{32,36}... | collective-permute-start | bytes 786440 | tf_op jit(solution)/shard_map/ppermute | solution.py:15
  24.8 10.2 %copy-start.16 = (bf16[1,256,512]{1,2,0:T(8,128)(2,1)}, bf16[1,256,512]{1,2,0:T(8,128)(2,1)S(1)}, u32[]{:S(2)}) copy-start(bf16[1,256,512]{1,2,0:T(8,128)(2,1)S(1)} %copy.69) | copy-start | bytes 786436
  25.1 4.2 copy-start.12
  25.2 8.5 %copy-start.5 = (bf16[1,256,512]{1,2,0:T(8,128)(2,1)}, bf16[1,256,512]{1,2,0:T(8,128)(2,1)S(1)}, u32[]{:S(2)}) copy-start(bf16[1,256,512]{1,2,0:T(8,128)(2,1)S(1)} %copy.99) | copy-start | bytes 786436
  28.0 5.7 %copy-start.14 = (bf16[256,4,128]{2,0,1:T(8,128)(2,1)}, bf16[256,4,128]{2,0,1:T(8,128)(2,1)S(1)}, u32[]{:S(2)}) copy-start(bf16[256,4,128]{2,0,1:T(8,128)(2,1)S(1)} %copy.68) | copy-start | bytes 786436
  29.3 4.4 copy-start.15
  34.8 2.1 copy-start.18
  35.0 1.9 copy-start.20
  36.9 1.1 copy-start.2
  39.6 2.3 copy-start.17
  39.8 2.2 copy-start.10
  39.8 2.2 copy-start.19
  39.8 2.2 copy-start.21
  42.0 4.6 copy-start.6
  45.4 1.2 copy-start.3
  46.6 1.0 copy-start.9
  51.1 13.7 %copy-start.4 = (bf16[4,256,768]{1,2,0:T(8,128)(2,1)S(1)}, bf16[4,256,768]{1,2,0:T(8,128)(2,1)}, u32[]{:S(2)}) copy-start(bf16[4,256,768]{1,2,0:T(8,128)(2,1)} %copy-done.3) | copy-start | bytes 4718596
  52.0 12.8 %copy-start.13 = (bf16[256,4,128]{2,0,1:T(8,128)(2,1)S(1)}, bf16[256,4,128]{2,0,1:T(8,128)(2,1)}, u32[]{:S(2)}) copy-start(bf16[256,4,128]{2,0,1:T(8,128)(2,1)} %copy-done.12) | copy-start | bytes 786436
  57.4 11.4 %copy-start.7 = (bf16[256,4,128]{0,2,1:T(8,128)(2,1)S(1)}, bf16[256,4,128]{0,2,1:T(8,128)(2,1)}, u32[]{:S(2)}) copy-start(bf16[256,4,128]{0,2,1:T(8,128)(2,1)} %get-tuple-element.27) | copy-start | bytes 786436
  57.4 11.5 %copy-start.8 = (bf16[256,4,128]{0,2,1:T(8,128)(2,1)S(1)}, bf16[256,4,128]{0,2,1:T(8,128)(2,1)}, u32[]{:S(2)}) copy-start(bf16[256,4,128]{0,2,1:T(8,128)(2,1)} %get-tuple-element.24) | copy-start | bytes 786436
  57.4 17.5 %collective-permute-start.4 = (bf16[256,512]{1,0:T(8,128)(2,1)}, bf16[256,512]{1,0:T(8,128)(2,1)}, u32[]{:S(2)}, u32[]{:S(2)}) collective-permute-start(bf16[256,512]{1,0:T(8,128)(2,1)} %copy.83), channel_id=1, source_target_pairs={{4,0},{8,4},{12,8},{16,12},{20,16},{24,20},{28,24},{32,28},{36,32}... | collective-permute-start | bytes 786440 | tf_op jit(solution)/shard_map/ppermute | solution.py:15
  60.3 9.6 %collective-permute-start.6 = (bf16[256,512]{1,0:T(8,128)(2,1)}, bf16[256,512]{1,0:T(8,128)(2,1)}, u32[]{:S(2)}, u32[]{:S(2)}) collective-permute-start(bf16[256,512]{1,0:T(8,128)(2,1)} %copy.88), channel_id=1, source_target_pairs={{4,0},{8,4},{12,8},{16,12},{20,16},{24,20},{28,24},{32,28},{36,32}... | collective-permute-start | bytes 786440 | tf_op jit(solution)/shard_map/ppermute | solution.py:15
  62.2 10.9 %collective-permute-start.7 = (bf16[256,512]{1,0:T(8,128)(2,1)}, bf16[256,512]{1,0:T(8,128)(2,1)}, u32[]{:S(2)}, u32[]{:S(2)}) collective-permute-start(bf16[256,512]{1,0:T(8,128)(2,1)} %copy.89), channel_id=1, source_target_pairs={{8,0},{12,4},{16,8},{20,12},{24,16},{28,20},{32,24},{36,28},{40,32... | collective-permute-start | bytes 786440 | tf_op jit(solution)/shard_map/ppermute | solution.py:15
  63.5 15.4 %collective-permute-start.5 = (bf16[256,512]{1,0:T(8,128)(2,1)}, bf16[256,512]{1,0:T(8,128)(2,1)}, u32[]{:S(2)}, u32[]{:S(2)}) collective-permute-start(bf16[256,512]{1,0:T(8,128)(2,1)} %copy.84), channel_id=1, source_target_pairs={{8,0},{12,4},{16,8},{20,12},{24,16},{28,20},{32,24},{36,28},{40,32... | collective-permute-start | bytes 786440 | tf_op jit(solution)/shard_map/ppermute | solution.py:15
Sparse Core Ops, SparseCore 0:
  49.5 479.2 all-reduce.1
where the time goes:
time: 538 us; the launch traced here: 537 us
  waiting for transfers between devices  456 us (85%)
  starting transfers between devices  20.8 us (4%)
  local copies, waits for them, and re-layouts  19.8 us (4%)
  matrix products  17.1 us (3%)
  between operations  14.5 us (3%)
  other arithmetic  8.87 us (2%)
    psum x1, waiting for transfers between devices, local(): summed = lax.psum(local_term, ('seq', 'dp'))  448 us
    ppermute x8, starting transfers between devices, shifted(): return lax.ppermute(array, axis, pairs)  20.7 us
  transfers between devices with their start and end apart: 9, of which 4 were waited for; matrix products, arithmetic and copies ran while one was open for 5% of the time, Pallas kernels for 0%

commit v1 on v0

v1 whole, which is shorter than its diff:
```python
import jax
import jax.numpy as jnp
from jax import lax
from jax.experimental import pallas as pl
from jax.experimental.pallas import tpu as pltpu
from jax.sharding import PartitionSpec as P

MESH = pl.DeviceIdType.MESH
EPS = 1e-05
HEADS = 4
HEAD_DIM = 128
ROWS = 256
WIDTH = 512
MODEL = 1024
NX = 4
NZ = 16
NY = 4
N_SEQ = 128
BAND = 2
PARTS = 2
PART = ROWS // PARTS
SCALE = 1.0 / ((BAND + 1) * ROWS)
BF16 = jnp.bfloat16
F32 = jnp.float32
NT = (((1,), (1,)), ((), ()))
TN = (((0,), (0,)), ((), ()))


def dot(a, b):
    return jnp.dot(a, b, preferred_element_type=F32)


def dot_nt(a, b):
    return lax.dot_general(a, b, NT, preferred_element_type=F32)


def dot_tn(a, b):
    return lax.dot_general(a, b, TN, preferred_element_type=F32)


def loop(n, body):
    lax.fori_loop(0, n, lambda i, c: (body(i), c)[1], jnp.int32(0))


def kernel(
    len_in, pat_in, q_in, k_in, v_in, gate_in, w_in, og_in,
    dq_out, dk_out, dv_out, dg_out, wg_out,
    len_ref, pat_ref, q3, kb, vb, gb, ogb, wb, mask, half, dgt, mix,
    ps, mr, d3, dsend, es, er, attn, slope, gt,
    gown, gs, gr, ya, yar, yb, ybr, xs, xr, zs, zr, tiles,
    dqa, dka, dva, dqo, dko, dvo, dgo,
    ld_sem, few_sem, out_sem, q_ss, q_rs, m_ss, m_rs, d_ss, d_rs, e_ss, e_rs,
    p_ss, p_rs, ya_ss, ya_rs, yb_ss, yb_rs, x_ss, x_rs, z_ss, z_rs, t_ss, t_rs,
):
    s = lax.axis_index("seq")
    y = lax.axis_index("dp")
    core = lax.rem(s, 2)
    x = lax.rem(s // 2, NX)
    z = s // (2 * NX)
    sib = s + 1 - 2 * core
    heads = range(HEADS)
    far = (2, 1)

    def ring(by):
        return lax.rem(s + by + N_SEQ, N_SEQ)

    def x_of(k):
        return lax.rem(x + k, NX)

    def at_x(k):
        return z * (2 * NX) + x_of(k) * 2 + core

    def at_z(m):
        return lax.rem(z + m, NZ) * (2 * NX) + x * 2 + core

    def at_y(j):
        return lax.rem(y + j, NY)

    barrier = pltpu.get_barrier_semaphore()

    def greet(seq, dp):
        pl.semaphore_signal(barrier, inc=1, device_id={"seq": seq, "dp": dp}, device_id_type=MESH)

    for by in (-2, -1, 1, 2):
        greet(ring(by), y)
    for j in range(1, NY):
        greet(s, at_y(j))
        greet(sib, at_y(j))
    for k in range(1, NX):
        greet(at_x(k), y)
    loop(NZ - 1, lambda m: greet(at_z(m + 1), y))

    def cols(h):
        return slice(h * HEAD_DIM, (h + 1) * HEAD_DIM)

    q_loads = [pltpu.make_async_copy(q_in.at[0, :, cols(h)], q3.at[h, 0], ld_sem.at[0, h]) for h in heads]
    k_loads = [pltpu.make_async_copy(k_in.at[0, :, cols(h)], kb.at[h], ld_sem.at[1, h]) for h in heads]
    v_loads = [pltpu.make_async_copy(v_in.at[0, :, cols(h)], vb.at[h], ld_sem.at[2, h]) for h in heads]
    gate_loads = [pltpu.make_async_copy(gate_in.at[0, :, cols(h)], gb.at[h], ld_sem.at[3, h]) for h in heads]
    og_loads = [
        pltpu.make_async_copy(og_in.at[0, :, cols(i)], ogb.at[i], ld_sem.at[4, i]) for i in range(2 * HEADS)
    ]
    w_load = pltpu.make_async_copy(w_in, wb, few_sem.at[0])
    few_loads = [pltpu.make_async_copy(len_in, len_ref, few_sem.at[1]), pltpu.make_async_copy(pat_in, pat_ref, few_sem.at[2])]
    for load in q_loads + k_loads + few_loads + v_loads + og_loads + [w_load] + gate_loads:
        load.start()

    def send(src, dst, ss, rs, seq, dp):
        return pltpu.make_async_remote_copy(
            src_ref=src, dst_ref=dst, send_sem=ss, recv_sem=rs,
            device_id={"seq": seq, "dp": dp}, device_id_type=MESH,
        )

    def rows_of(r):
        return pl.ds(r * PART, PART)

    def band_copy(src, dst, ss, rs, t, h, r, by):
        return send(src.at[rows_of(r)], dst.at[rows_of(r)], ss.at[t - 1, h, r], rs.at[t - 1, h, r], ring(by), y)

    def q_copy(t, h, r):
        return band_copy(q3.at[h, 0], q3.at[h, t], q_ss, q_rs, t, h, r, -t)

    def m_copy(t, h, r):
        return band_copy(ps.at[h, t - 1], mr.at[h, t - 1], m_ss, m_rs, t, h, r, t)

    def d_copy(t, h, r):
        return band_copy(dsend.at[h, t - 1], d3.at[h, t], d_ss, d_rs, t, h, r, -t)

    def e_copy(t, h, r):
        return band_copy(es.at[h, t - 1], er.at[h, t - 1], e_ss, e_rs, t, h, r, t)

    q_loads[0].wait()
    pl.semaphore_wait(barrier, 4 + 2 * (NY - 1) + (NX - 1) + (NZ - 1))
    for r in range(PARTS):
        for h in heads:
            if h and not r:
                q_loads[h].wait()
            for t in far:
                q_copy(t, h, r).start()

    for load in few_loads:
        load.wait()
    ends = []
    total = jnp.int32(0)
    for i in range(len_ref.shape[1]):
        total = total + len_ref[0, i]
        ends.append(total)

    def doc(at):
        number = jnp.zeros(at.shape, jnp.int32)
        for end in ends:
            number = number + jnp.where(at >= end, 1, 0)
        return number

    key_at = s * ROWS + lax.broadcasted_iota(jnp.int32, (1, ROWS), 1)
    key_doc = doc(key_at)
    for t in range(BAND + 1):
        query_at = (s + t) * ROWS + lax.broadcasted_iota(jnp.int32, (ROWS, 1), 0)
        keep = (doc(query_at) == key_doc) & (key_at <= query_at)
        mask[t] = jnp.where(keep, SCALE, 0.0).astype(F32)
        half[t] = jnp.where(keep, 0.5 * SCALE, 0.0).astype(F32)

    own = slice(0, 1)
    both = pl.ds(1, BAND)

    def flat(array):
        return array.reshape(-1, array.shape[-1])

    def forward(ts, rows, h):
        shape = (1 if ts is own else BAND, rows.size, ROWS)
        scores = dot_nt(flat(q3[h, ts, rows]), kb[h])
        middle = 0.5 * scores
        tanh = jnp.tanh(middle)
        twice = 1.0 + tanh
        silu = middle * twice
        a = (silu * flat(mask[ts, rows])).astype(BF16)
        attn[h, ts, rows] = a.reshape(shape)
        slope[h, ts, rows] = ((twice + silu * (1.0 - tanh)) * flat(half[ts, rows])).reshape(shape)
        return dot(a, vb[h])

    for load in k_loads + v_loads:
        load.wait()
    for h in heads:
        mix[h] = forward(own, pl.ds(0, ROWS), h)

    for load in og_loads:
        load.wait()
    w_load.wait()
    og = jnp.concatenate([ogb[i] for i in range(2 * HEADS)], axis=1)
    for i in range(2):
        part = dot_nt(og, wb[pl.ds(i * 256, 256), :])
        dgt[2 * i] = part[:, :HEAD_DIM]
        dgt[2 * i + 1] = part[:, HEAD_DIM:]
    for load in gate_loads:
        load.wait()

    def far_forward(h, r):
        for t in far:
            q_copy(t, h, r).wait_recv()
        ps[h, :, rows_of(r)] = forward(both, rows_of(r), h).astype(BF16).reshape(BAND, PART, HEAD_DIM)
        for t in far:
            m_copy(t, h, r).start()

    near = [jnp.where(pat_ref[0, 0, t] > 0, 1.0, 0.0).astype(F32) for t in range(BAND)]

    step_rows = 64

    def norm(rows):
        def mean(parts):
            return jnp.sum(sum(parts[1:], parts[0]), axis=1, keepdims=True) * (1.0 / WIDTH)

        mixed = [
            mix[h, rows] + near[0] * mr[h, 0, rows].astype(F32) + near[1] * mr[h, 1, rows].astype(F32) for h in heads
        ]
        centre = mean(mixed)
        mixed = [m - centre for m in mixed]
        inv = lax.rsqrt(mean([m * m for m in mixed]) + EPS)
        normed = [m * inv for m in mixed]
        grad = []
        gated = []
        for h in heads:
            gate = gb[h, rows].astype(F32)
            gated.append((normed[h] * gate).astype(BF16))
            up = dgt[h, rows]
            dgo[rows, cols(h)] = (up * normed[h]).astype(BF16)
            grad.append(up * gate)
        first = mean(grad)
        second = mean([g * n for g, n in zip(grad, normed)])
        for h in heads:
            down = (inv * (grad[h] - first - normed[h] * second)).astype(BF16)
            d3[h, 0, rows] = down
            for t in range(BAND):
                dsend[h, t, rows] = (near[t] * down.astype(F32)).astype(BF16)

        return jnp.concatenate(gated, axis=1)

    def norm_part(r):
        for h in heads:
            for t in far:
                m_copy(t, h, r).wait_recv()
        gated = [norm(pl.ds(r * PART + i * step_rows, step_rows)) for i in range(PART // step_rows)]
        for h in heads:
            for t in far:
                d_copy(t, h, r).start()
        gated = jnp.concatenate(gated, axis=0)
        gt[:, :, :, rows_of(r)] = gated.T.astype(F32).reshape(NZ, NX, 8, PART)

    def backward(ts, rows, h):
        q = flat(q3[h, ts, rows])
        d = flat(d3[h, ts, rows])
        ds = (dot_nt(d, vb[h]) * flat(slope[h, ts, rows])).astype(BF16)
        return dot(ds, kb[h]), dot_tn(ds, q), dot_tn(flat(attn[h, ts, rows]), d)

    def own_backward(r):
        for h in heads:
            dq, dk, dv = backward(own, rows_of(r), h)
            dqa[h, rows_of(r)] = dq
            dka[h] = dk if r == 0 else dka[h] + dk
            dva[h] = dv if r == 0 else dva[h] + dv

    def far_backward(h, r):
        for t in far:
            d_copy(t, h, r).wait_recv()
        dq, dk, dv = backward(both, rows_of(r), h)
        es[h, :, rows_of(r)] = dq.astype(BF16).reshape(BAND, PART, HEAD_DIM)
        for t in far:
            e_copy(t, h, r).start()
        if r < PARTS - 1:
            dka[h] = dka[h] + dk
            dva[h] = dva[h] + dv
        else:
            dko[:, cols(h)] = (dka[h] + dk).astype(BF16)
            dvo[:, cols(h)] = (dva[h] + dv).astype(BF16)

    for h in heads:
        far_forward(h, 0)
    far_forward(0, 1)
    far_forward(1, 1)
    norm_part(0)
    far_forward(2, 1)
    far_forward(3, 1)
    own_backward(0)
    norm_part(1)

    piece = NZ * 8
    cut = piece // 2
    low = slice(0, cut)
    high = slice(cut, piece)
    up = at_y(1)
    down = at_y(NY - 1)
    across = at_y(2)

    def p_copy(k):
        return send(gs.at[k], gr.at[k], p_ss.at[k], p_rs.at[k], sib, y)

    def ya_copy(k, i):
        return send(ya.at[k, i], yar.at[k, i], ya_ss.at[k, i], ya_rs.at[k, i], s, (up, down)[i])

    def yb_copy(k, i):
        return send(yb.at[k, i], ybr.at[k, i], yb_ss.at[k, i], yb_rs.at[k, i], s, (up, down)[i])

    def x_copy(k):
        return send(xs.at[k], xr.at[k], x_ss.at[k], x_rs.at[k], at_x(k), y)

    order = (2, 1, 3, 0)
    other = jnp.concatenate([ogb[(1 - core) * 4 + i] for i in range(NY)], axis=1)
    for k in order:
        part = dot(gt[:, x_of(k)].reshape(piece, ROWS).astype(BF16), other)
        for i in range(NY):
            gs[k, i] = part[:, cols(i)].astype(BF16)
        p_copy(k).start()
    mine = jnp.concatenate([ogb[core * 4 + i] for i in range(NY)], axis=1)
    for k in order:
        part = dot(gt[:, x_of(k)].reshape(piece, ROWS).astype(BF16), mine)
        for i in range(NY):
            gown[k, i] = part[:, cols(i)]

    for k in order:
        p_copy(k).wait_recv()
        for i in range(NY):
            gown[k, i] = gown[k, i] + gr[k, i].astype(F32)
        ya[k, 0] = gown[k, across, low].astype(BF16)
        ya[k, 1] = gown[k, across, high].astype(BF16)
        for i in range(2):
            ya_copy(k, i).start()

    def y_pass(k):
        for i in range(2):
            ya_copy(k, i).wait_recv()
        yb[k, 0, low] = (gown[k, up, low] + yar[k, 0].astype(F32)).astype(BF16)
        yb[k, 0, high] = gown[k, up, high].astype(BF16)
        yb[k, 1, low] = gown[k, down, low].astype(BF16)
        yb[k, 1, high] = (gown[k, down, high] + yar[k, 1].astype(F32)).astype(BF16)
        for i in range(2):
            yb_copy(k, i).start()

    gate_out = pltpu.make_async_copy(dgo, dg_out.at[0], out_sem.at[0])
    gate_out.start()

    def y_sum(k):
        for i in range(2):
            yb_copy(k, i).wait_recv()
        return gown[k, y] + ybr[k, 0].astype(F32) + ybr[k, 1].astype(F32)

    def x_start(k):
        xs[k] = y_sum(k).astype(BF16)
        x_copy(k).start()

    far_backward(0, 0)
    far_backward(1, 0)
    y_pass(2)
    y_pass(1)
    far_backward(2, 0)
    y_pass(3)
    y_pass(0)
    far_backward(3, 0)
    own_backward(1)
    x_start(2)
    far_backward(0, 1)
    x_start(1)
    far_backward(1, 1)
    x_start(3)

    z_order = (8, 7, 9, 6, 10, 5, 11, 4, 12, 3, 13, 2, 14, 1, 15)

    def z_copy(m):
        return send(zs.at[lax.rem(z + m, NZ)], zr.at[m], z_ss.at[m], z_rs.at[m], at_z(m), y)

    plane = y_sum(0)
    for k in range(1, NX):
        x_copy(k).wait_recv()
        plane = plane + xr[k].astype(F32)
    zs[...] = plane.reshape(NZ, 8, 128)
    for m in z_order:
        z_copy(m).start()

    far_backward(2, 1)
    far_backward(3, 1)
    key_out = pltpu.make_async_copy(dko, dk_out.at[0], out_sem.at[1])
    value_out = pltpu.make_async_copy(dvo, dv_out.at[0], out_sem.at[2])
    key_out.start()
    value_out.start()

    def t_copy(dy, dc):
        slot = core * NY + y
        seq = s if dc == 0 else sib
        return send(tiles.at[slot], tiles.at[slot], t_ss.at[dy * 2 + dc], t_rs.at[slot], seq, at_y(dy))

    others = [(dy, dc) for dy in range(NY) for dc in range(2) if (dy, dc) != (0, 0)]

    for m in z_order:
        z_copy(m).wait_recv()
    tile = zs[z]
    for m in range(1, NZ):
        tile = tile + zr[m]
    tiles[core * NY + y] = tile
    for dy, dc in others:
        t_copy(dy, dc).start()

    for h in heads:
        for r in range(PARTS):
            for t in far:
                e_copy(t, h, r).wait_recv()
        dqo[:, cols(h)] = (dqa[h] + er[h, 0].astype(F32) + er[h, 1].astype(F32)).astype(BF16)
    query_out = pltpu.make_async_copy(dqo, dq_out.at[0], out_sem.at[3])
    query_out.start()

    for dy, dc in others:
        slot = (core if dc == 0 else 1 - core) * NY + at_y(dy)
        send(tiles.at[slot], tiles.at[slot], t_ss.at[dy * 2 + dc], t_rs.at[slot], s, y).wait_recv()
    lower = jnp.broadcast_to(core, (4, 128)) == 0
    for slot in range(2 * NY):
        full = tiles[slot]
        wg_out[:, slot * 128:(slot + 1) * 128] = jnp.where(lower, full[:4], full[4:])

    for h in heads:
        for t in far:
            for r in range(PARTS):
                for copy in (q_copy, m_copy, d_copy, e_copy):
                    copy(t, h, r).wait_send()
    for k in range(NX):
        p_copy(k).wait_send()
        for i in range(2):
            ya_copy(k, i).wait_send()
            yb_copy(k, i).wait_send()
        if k:
            x_copy(k).wait_send()
    for m in z_order:
        z_copy(m).wait_send()
    for dy, dc in others:
        t_copy(dy, dc).wait_send()
    for out in (gate_out, key_out, value_out, query_out):
        out.wait()


def finish(*refs):
    sem = refs[-1]
    n = len(refs) // 2
    copies = [pltpu.make_async_copy(refs[i], refs[n + i], sem.at[i]) for i in range(n)]
    for copy in copies:
        copy.start()
    for copy in copies:
        copy.wait()


def finished(arrays):
    anywhere = pl.BlockSpec(memory_space=pl.ANY)
    return pl.pallas_call(
        finish,
        out_shape=tuple(jax.ShapeDtypeStruct(a.shape, a.dtype) for a in arrays),
        in_specs=[pl.BlockSpec(memory_space=pltpu.VMEM)] * len(arrays),
        out_specs=(anywhere,) * len(arrays),
        scratch_shapes=[pltpu.SemaphoreType.DMA((len(arrays),))],
        compiler_params=pltpu.CompilerParams(vmem_limit_bytes=16 * 1024 * 1024),
    )(*arrays)


def local(queries, keys, values, gates, out_weight, out_grad, lengths, pattern):
    block = (HEADS, ROWS, HEAD_DIM)
    two = (HEADS, BAND, ROWS, HEAD_DIM)
    three = (HEADS, BAND + 1, ROWS, HEAD_DIM)
    band = (BAND + 1, ROWS, ROWS)
    rows = (ROWS, WIDTH)
    vmem = pltpu.VMEM
    smem = pltpu.SMEM
    scratch = [
        smem(lengths.shape, jnp.int32), smem(pattern.shape, jnp.int32),
        vmem(three, BF16), vmem(block, BF16), vmem(block, BF16), vmem(block, BF16),
        vmem((2 * HEADS, ROWS, HEAD_DIM), BF16), vmem((WIDTH, MODEL), BF16),
        vmem(band, F32), vmem(band, F32), vmem(block, F32), vmem(block, F32),
        vmem(two, BF16), vmem(two, BF16),
        vmem(three, BF16), vmem(two, BF16), vmem(two, BF16), vmem(two, BF16),
        vmem((HEADS,) + band, BF16), vmem((HEADS,) + band, F32),
        vmem((NZ, NX, 8, ROWS), F32),
        vmem((NX, NY, NZ * 8, 128), F32), vmem((NX, NY, NZ * 8, 128), BF16), vmem((NX, NY, NZ * 8, 128), BF16),
        vmem((NX, 2, NZ * 4, 128), BF16), vmem((NX, 2, NZ * 4, 128), BF16),
        vmem((NX, 2, NZ * 8, 128), BF16), vmem((NX, 2, NZ * 8, 128), BF16),
        vmem((NX, NZ * 8, 128), BF16), vmem((NX, NZ * 8, 128), BF16),
        vmem((NZ, 8, 128), F32), vmem((NZ, 8, 128), F32), vmem((2 * NY, 8, 128), F32),
        vmem(block, F32), vmem(block, F32), vmem(block, F32),
        vmem(rows, BF16), vmem(rows, BF16), vmem(rows, BF16), vmem(rows, BF16),
    ]
    dma = pltpu.SemaphoreType.DMA
    scratch += [dma((5, 2 * HEADS)), dma((3,)), dma((4,))]
    scratch += [dma((BAND, HEADS, PARTS))] * 8
    scratch += [dma((NX,))] * 2 + [dma((NX, 2))] * 4 + [dma((NX,))] * 2 + [dma((NZ,))] * 2 + [dma((2 * NY,))] * 2
    anywhere = pl.BlockSpec(memory_space=pl.ANY)
    grad = jax.ShapeDtypeStruct((1, ROWS, WIDTH), BF16)
    operands = (lengths, pattern, queries, keys, values, gates, out_weight, out_grad)
    results = pl.pallas_call(
        kernel,
        out_shape=(grad, grad, grad, grad, jax.ShapeDtypeStruct((WIDTH // N_SEQ, MODEL), F32)),
        in_specs=[anywhere] * len(operands),
        out_specs=(anywhere,) * 4 + (pl.BlockSpec(memory_space=pltpu.VMEM),),
        scratch_shapes=scratch,
        compiler_params=pltpu.CompilerParams(
            collective_id=0, has_side_effects=True, vmem_limit_bytes=40 * 1024 * 1024
        ),
        cost_estimate=pl.CostEstimate(flops=2 * 10**9, bytes_accessed=5 * 2**20, transcendentals=3 * 4 * ROWS * ROWS),
    )(*[pltpu.with_memory_space_constraint(a, pltpu.HBM) for a in operands])
    return finished(results)


def solution(mesh):
    events = P("dp", "seq", None)
    return jax.shard_map(
        local,
        mesh=mesh,
        in_specs=(events, events, events, events, P(), events, P("dp", None), events),
        out_specs=(events, events, events, events, P("seq", None)),
        check_vma=False,
    )
```

time: 538 us -> 62.4 us (0.12)
  waiting for transfers between devices: 456 us -> 0 us
  Pallas kernels: 0 us -> 61.7 us
  starting transfers between devices: 20.8 us -> 0 us
  local copies, waits for them, and re-layouts: 19.8 us -> 0 us
  matrix products: 17.1 us -> 0 us
  between operations: 14.5 us -> 0.64 us
  other arithmetic: 8.87 us -> 0 us
    psum x1 -> x0, waiting for transfers between devices: 448 us -> none  [local(): summed = lax.psum(local_term, ('seq', 'dp'))]
    pallas_call x0 -> x2, Pallas kernels: none -> 61.7 us  [the longest x1 60.6 us: local(): pl.pallas_call(kernel, out_shape=(grad, grad, grad, grad, jax.ShapeDtypeS...]
    ppermute x8 -> x0, starting transfers between devices: 20.7 us -> none  [shifted(): return lax.ppermute(array, axis, pairs)]
    dot_general x8 -> x0, matrix products: 17.1 us -> none  [the longest x1 4.4 us: local(): jnp.einsum('qhd,khd->hqk', query_heads, key_band, preferred_element_type=...]
    ppermute x8 -> x0, waiting for transfers between devices: 8.01 us -> none  [shifted(): return lax.ppermute(array, axis, pairs)]
    squeeze x4 -> x0, local copies, waits for them, and re-layouts: 6.31 us -> none  [the longest x2 3.65 us: local(): value_terms[offset]]
    unnamed x47 -> x0, local copies, waits for them, and re-layouts: 5.64 us -> none
  transfers between devices with their start and end apart: 9 -> 0, of which waited for: 4 -> 0; matrix products, arithmetic and copies ran while one was open for 5% -> 0% of each run, Pallas kernels for 0% -> 0%
where the time goes in v1:
time: 62.4 us; the launch traced here: 62.3 us
  Pallas kernels  61.7 us (99%)
  between operations  0.64 us (1%)
    pallas_call x1, Pallas kernels, local(): pl.pallas_call(kernel, out_shape=(grad, grad, grad, grad, jax.ShapeDtypeS...  60.6 us

profile of v1, /device:TPU:1, one launch (start us, length us, event | category | flops | bytes accessed | tf_op | source)
XLA Modules:
  0.0 62.3 jit_solution(6891490706878368841)
XLA Ops:
  0.6 60.6 %shard_map.119 = (bf16[1,256,512]{2,1,0:T(8,128)(2,1)S(1)}, bf16[1,256,512]{2,1,0:T(8,128)(2,1)S(1)}, bf16[1,256,512]{2,1,0:T(8,128)(2,1)S(1)}, bf16[1,256,512]{2,1,0:T(8,128)(2,1)S(1)}, f32[4,1024]{1,0:T(4,128)S(1)}) custom-call(s32[1,4]{1,0:T(1,128)} %len_in.1, s32[1,1,2]{2,1,0:T(1,128)} %pat_in.1, bf16[1,256,512]{2,1,0:T(8,128)(2,1)} %q_in.1, ...), custom_call_target="tpu_custom_call" | custom-call | flops 2000000000 | bytes 5242880 | tf_op jit(solution)/shard_map/pallas_call | solution.py:490
  61.3 1.0 %shard_map.120 = (bf16[1,256,512]{2,1,0:T(8,128)(2,1)}, bf16[1,256,512]{2,1,0:T(8,128)(2,1)}, bf16[1,256,512]{2,1,0:T(8,128)(2,1)}, bf16[1,256,512]{2,1,0:T(8,128)(2,1)}, f32[4,1024]{1,0:T(4,128)}) custom-call(bf16[1,256,512]{2,1,0:T(8,128)(2,1)S(1)} %get-tuple-element.10.refs_0_, bf16[1,256,512]{2,1,0:T(8,128)(2,1)S(1)} %get-tuple-element.11.refs_1_, ...), custom_call_target="tpu_custom_call" | custom-call | tf_op jit(solution)/shard_map/pallas_call | solution.py:448

commit v2 on v1

--- a/solution.py
+++ b/solution.py
@@ -45,11 +45,11 @@
 def kernel(
     len_in, pat_in, q_in, k_in, v_in, gate_in, w_in, og_in,
     dq_out, dk_out, dv_out, dg_out, wg_out,
-    len_ref, pat_ref, q3, kb, vb, gb, ogb, wb, mask, half, dgt, mix,
-    ps, mr, d3, dsend, es, er, attn, slope, gt,
+    len_ref, pat_ref, q3, kb, vb, gb, ogb, wb, kt, vt, mask, half, dgt, mix,
+    ps, mr, d3, dsend, es, er, attn_own, attn_far, qt_own, qt_far, slope_own, slope_far, gt,
     gown, gs, gr, ya, yar, yb, ybr, xs, xr, zs, zr, tiles,
     dqa, dka, dva, dqo, dko, dvo, dgo,
-    ld_sem, few_sem, out_sem, q_ss, q_rs, m_ss, m_rs, d_ss, d_rs, e_ss, e_rs,
+    ld_sem, out_sem, q_ss, q_rs, m_ss, m_rs, d_ss, d_rs, e_ss, e_rs,
     p_ss, p_rs, ya_ss, ya_rs, yb_ss, yb_rs, x_ss, x_rs, z_ss, z_rs, t_ss, t_rs,
 ):
     s = lax.axis_index("seq")
@@ -81,28 +81,29 @@
     def greet(seq, dp):
         pl.semaphore_signal(barrier, inc=1, device_id={"seq": seq, "dp": dp}, device_id_type=MESH)
 
+    def cols(h):
+        return slice(h * HEAD_DIM, (h + 1) * HEAD_DIM)
+
     for by in (-2, -1, 1, 2):
         greet(ring(by), y)
+    q_loads = [pltpu.make_async_copy(q_in.at[0, :, cols(h)], q3.at[h, 0], ld_sem.at[h]) for h in heads]
+    for load in q_loads:
+        load.start()
     for j in range(1, NY):
         greet(s, at_y(j))
         greet(sib, at_y(j))
     for k in range(1, NX):
         greet(at_x(k), y)
-    loop(NZ - 1, lambda m: greet(at_z(m + 1), y))
-
-    def cols(h):
-        return slice(h * HEAD_DIM, (h + 1) * HEAD_DIM)
-
-    q_loads = [pltpu.make_async_copy(q_in.at[0, :, cols(h)], q3.at[h, 0], ld_sem.at[0, h]) for h in heads]
-    k_loads = [pltpu.make_async_copy(k_in.at[0, :, cols(h)], kb.at[h], ld_sem.at[1, h]) for h in heads]
-    v_loads = [pltpu.make_async_copy(v_in.at[0, :, cols(h)], vb.at[h], ld_sem.at[2, h]) for h in heads]
-    gate_loads = [pltpu.make_async_copy(gate_in.at[0, :, cols(h)], gb.at[h], ld_sem.at[3, h]) for h in heads]
-    og_loads = [
-        pltpu.make_async_copy(og_in.at[0, :, cols(i)], ogb.at[i], ld_sem.at[4, i]) for i in range(2 * HEADS)
-    ]
-    w_load = pltpu.make_async_copy(w_in, wb, few_sem.at[0])
-    few_loads = [pltpu.make_async_copy(len_in, len_ref, few_sem.at[1]), pltpu.make_async_copy(pat_in, pat_ref, few_sem.at[2])]
-    for load in q_loads + k_loads + few_loads + v_loads + og_loads + [w_load] + gate_loads:
+    for m in range(1, NZ):
+        greet(at_z(m), y)
+
+    k_load = pltpu.make_async_copy(k_in.at[0], kb, ld_sem.at[4])
+    v_load = pltpu.make_async_copy(v_in.at[0], vb, ld_sem.at[5])
+    gate_load = pltpu.make_async_copy(gate_in.at[0], gb, ld_sem.at[6])
+    og_load = pltpu.make_async_copy(og_in.at[0], ogb, ld_sem.at[7])
+    w_load = pltpu.make_async_copy(w_in, wb, ld_sem.at[8])
+    few_loads = [pltpu.make_async_copy(len_in, len_ref, ld_sem.at[9]), pltpu.make_async_copy(pat_in, pat_ref, ld_sem.at[10])]
+    for load in [k_load, v_load] + few_loads + [og_load, w_load, gate_load]:
         load.start()
 
     def send(src, dst, ss, rs, seq, dp):
@@ -114,20 +115,26 @@
     def rows_of(r):
         return pl.ds(r * PART, PART)
 
-    def band_copy(src, dst, ss, rs, t, h, r, by):
-        return send(src.at[rows_of(r)], dst.at[rows_of(r)], ss.at[t - 1, h, r], rs.at[t - 1, h, r], ring(by), y)
+    def band_copy(src, dst, ss, rs, h, r, by):
+        return send(src.at[rows_of(r)], dst.at[rows_of(r)], ss.at[0], rs, ring(by), y)
 
     def q_copy(t, h, r):
-        return band_copy(q3.at[h, 0], q3.at[h, t], q_ss, q_rs, t, h, r, -t)
+        return band_copy(q3.at[h, 0], q3.at[h, t], q_ss, q_rs.at[h, r], h, r, -t)
 
     def m_copy(t, h, r):
-        return band_copy(ps.at[h, t - 1], mr.at[h, t - 1], m_ss, m_rs, t, h, r, t)
+        return band_copy(ps.at[h, t - 1], mr.at[h, t - 1], m_ss, m_rs.at[r], h, r, t)
 
     def d_copy(t, h, r):
-        return band_copy(dsend.at[h, t - 1], d3.at[h, t], d_ss, d_rs, t, h, r, -t)
+        return band_copy(dsend.at[h, t - 1], d3.at[h, t], d_ss, d_rs.at[h, r], h, r, -t)
 
     def e_copy(t, h, r):
-        return band_copy(es.at[h, t - 1], er.at[h, t - 1], e_ss, e_rs, t, h, r, t)
+        return band_copy(es.at[h, t - 1], er.at[h, t - 1], e_ss, e_rs.at[0], h, r, t)
+
+    def landed(ref, sem):
+        send(ref, ref, sem, sem, sib, y).wait_recv()
+
+    def sent(ref, sem):
+        send(ref, ref, sem, sem, sib, y).wait_send()
 
     q_loads[0].wait()
     pl.semaphore_wait(barrier, 4 + 2 * (NY - 1) + (NX - 1) + (NZ - 1))
@@ -167,39 +174,44 @@
         return array.reshape(-1, array.shape[-1])
 
     def forward(ts, rows, h):
-        shape = (1 if ts is own else BAND, rows.size, ROWS)
-        scores = dot_nt(flat(q3[h, ts, rows]), kb[h])
+        q = flat(q3[h, ts, rows])
+        scores = dot(q, kt[h])
         middle = 0.5 * scores
         tanh = jnp.tanh(middle)
         twice = 1.0 + tanh
         silu = middle * twice
         a = (silu * flat(mask[ts, rows])).astype(BF16)
-        attn[h, ts, rows] = a.reshape(shape)
-        slope[h, ts, rows] = ((twice + silu * (1.0 - tanh)) * flat(half[ts, rows])).reshape(shape)
-        return dot(a, vb[h])
-
-    for load in k_loads + v_loads:
-        load.wait()
+        slope = (twice + silu * (1.0 - tanh)) * flat(half[ts, rows])
+        return q, a, slope, dot(a, vb[:, cols(h)])
+
+    k_load.wait()
     for h in heads:
-        mix[h] = forward(own, pl.ds(0, ROWS), h)
-
-    for load in og_loads:
-        load.wait()
+        kt[h] = kb[:, cols(h)].T
+    v_load.wait()
+    for h in heads:
+        vt[h] = vb[:, cols(h)].T
+    for h in heads:
+        q, a, slope_own[h], mix[h] = forward(own, pl.ds(0, ROWS), h)
+        attn_own[h] = a.T
+        qt_own[h] = q.T
+
+    og_load.wait()
     w_load.wait()
-    og = jnp.concatenate([ogb[i] for i in range(2 * HEADS)], axis=1)
+    og = ogb[...]
     for i in range(2):
         part = dot_nt(og, wb[pl.ds(i * 256, 256), :])
         dgt[2 * i] = part[:, :HEAD_DIM]
         dgt[2 * i + 1] = part[:, HEAD_DIM:]
-    for load in gate_loads:
-        load.wait()
+    gate_load.wait()
 
     def far_forward(h, r):
-        for t in far:
-            q_copy(t, h, r).wait_recv()
-        ps[h, :, rows_of(r)] = forward(both, rows_of(r), h).astype(BF16).reshape(BAND, PART, HEAD_DIM)
+        landed(q3.at[h, both, rows_of(r)], q_rs.at[h, r])
+        q, a, slope_far[h, r], part = forward(both, rows_of(r), h)
+        ps[h, :, rows_of(r)] = part.astype(BF16).reshape(BAND, PART, HEAD_DIM)
         for t in far:
             m_copy(t, h, r).start()
+        attn_far[h, r] = a.T
+        qt_far[h, r] = q.T
 
     near = [jnp.where(pat_ref[0, 0, t] > 0, 1.0, 0.0).astype(F32) for t in range(BAND)]
 
@@ -219,7 +231,7 @@
         grad = []
         gated = []
         for h in heads:
-            gate = gb[h, rows].astype(F32)
+            gate = gb[rows, cols(h)].astype(F32)
             gated.append((normed[h] * gate).astype(BF16))
             up = dgt[h, rows]
             dgo[rows, cols(h)] = (up * normed[h]).astype(BF16)
@@ -235,9 +247,7 @@
         return jnp.concatenate(gated, axis=1)
 
     def norm_part(r):
-        for h in heads:
-            for t in far:
-                m_copy(t, h, r).wait_recv()
+        landed(mr.at[:, :, rows_of(r)], m_rs.at[r])
         gated = [norm(pl.ds(r * PART + i * step_rows, step_rows)) for i in range(PART // step_rows)]
         for h in heads:
             for t in far:
@@ -245,23 +255,21 @@
         gated = jnp.concatenate(gated, axis=0)
         gt[:, :, :, rows_of(r)] = gated.T.astype(F32).reshape(NZ, NX, 8, PART)
 
-    def backward(ts, rows, h):
-        q = flat(q3[h, ts, rows])
-        d = flat(d3[h, ts, rows])
-        ds = (dot_nt(d, vb[h]) * flat(slope[h, ts, rows])).astype(BF16)
-        return dot(ds, kb[h]), dot_tn(ds, q), dot_tn(flat(attn[h, ts, rows]), d)
+    def backward(d, slope, h, q_t, attn_t):
+        ds = (dot(d, vt[h]) * slope).astype(BF16)
+        return dot(ds, kb[:, cols(h)]), dot(q_t, ds), dot(attn_t, d)
 
     def own_backward(r):
+        lanes = slice(r * PART, (r + 1) * PART)
         for h in heads:
-            dq, dk, dv = backward(own, rows_of(r), h)
+            dq, dk, dv = backward(d3[h, 0, rows_of(r)], slope_own[h, rows_of(r)], h, qt_own[h, :, lanes], attn_own[h, :, lanes])
             dqa[h, rows_of(r)] = dq
             dka[h] = dk if r == 0 else dka[h] + dk
             dva[h] = dv if r == 0 else dva[h] + dv
 
     def far_backward(h, r):
-        for t in far:
-            d_copy(t, h, r).wait_recv()
-        dq, dk, dv = backward(both, rows_of(r), h)
+        landed(d3.at[h, both, rows_of(r)], d_rs.at[h, r])
+        dq, dk, dv = backward(flat(d3[h, both, rows_of(r)]), slope_far[h, r], h, qt_far[h, r], attn_far[h, r])
         es[h, :, rows_of(r)] = dq.astype(BF16).reshape(BAND, PART, HEAD_DIM)
         for t in far:
             e_copy(t, h, r).start()
@@ -269,7 +277,7 @@
             dka[h] = dka[h] + dk
             dva[h] = dva[h] + dv
         else:
-            dko[:, cols(h)] = (dka[h] + dk).astype(BF16)
+            dko[:, cols(h)] = (dka[h] + dk).T.astype(BF16)
             dvo[:, cols(h)] = (dva[h] + dv).astype(BF16)
 
     for h in heads:
@@ -291,25 +299,25 @@
     across = at_y(2)
 
     def p_copy(k):
-        return send(gs.at[k], gr.at[k], p_ss.at[k], p_rs.at[k], sib, y)
+        return send(gs.at[k], gr.at[k], p_ss.at[0], p_rs.at[k], sib, y)
 
     def ya_copy(k, i):
-        return send(ya.at[k, i], yar.at[k, i], ya_ss.at[k, i], ya_rs.at[k, i], s, (up, down)[i])
+        return send(ya.at[k, i], yar.at[k, i], ya_ss.at[0], ya_rs.at[k], s, (up, down)[i])
 
     def yb_copy(k, i):
-        return send(yb.at[k, i], ybr.at[k, i], yb_ss.at[k, i], yb_rs.at[k, i], s, (up, down)[i])
+        return send(yb.at[k, i], ybr.at[k, i], yb_ss.at[0], yb_rs.at[k], s, (up, down)[i])
 
     def x_copy(k):
-        return send(xs.at[k], xr.at[k], x_ss.at[k], x_rs.at[k], at_x(k), y)
+        return send(xs.at[k], xr.at[k], x_ss.at[0], x_rs.at[0], at_x(k), y)
 
     order = (2, 1, 3, 0)
-    other = jnp.concatenate([ogb[(1 - core) * 4 + i] for i in range(NY)], axis=1)
+    other = ogb[:, pl.ds(pl.multiple_of((1 - core) * WIDTH, WIDTH), WIDTH)]
     for k in order:
         part = dot(gt[:, x_of(k)].reshape(piece, ROWS).astype(BF16), other)
         for i in range(NY):
             gs[k, i] = part[:, cols(i)].astype(BF16)
         p_copy(k).start()
-    mine = jnp.concatenate([ogb[core * 4 + i] for i in range(NY)], axis=1)
+    mine = ogb[:, pl.ds(pl.multiple_of(core * WIDTH, WIDTH), WIDTH)]
     for k in order:
         part = dot(gt[:, x_of(k)].reshape(piece, ROWS).astype(BF16), mine)
         for i in range(NY):
@@ -325,8 +333,7 @@
             ya_copy(k, i).start()
 
     def y_pass(k):
-        for i in range(2):
-            ya_copy(k, i).wait_recv()
+        landed(yar.at[k], ya_rs.at[k])
         yb[k, 0, low] = (gown[k, up, low] + yar[k, 0].astype(F32)).astype(BF16)
         yb[k, 0, high] = gown[k, up, high].astype(BF16)
         yb[k, 1, low] = gown[k, down, low].astype(BF16)
@@ -338,8 +345,7 @@
     gate_out.start()
 
     def y_sum(k):
-        for i in range(2):
-            yb_copy(k, i).wait_recv()
+        landed(ybr.at[k], yb_rs.at[k])
         return gown[k, y] + ybr[k, 0].astype(F32) + ybr[k, 1].astype(F32)
 
     def x_start(k):
@@ -364,11 +370,11 @@
     z_order = (8, 7, 9, 6, 10, 5, 11, 4, 12, 3, 13, 2, 14, 1, 15)
 
     def z_copy(m):
-        return send(zs.at[lax.rem(z + m, NZ)], zr.at[m], z_ss.at[m], z_rs.at[m], at_z(m), y)
+        return send(zs.at[lax.rem(z + m, NZ)], zr.at[m], z_ss.at[0], z_rs.at[0], at_z(m), y)
 
     plane = y_sum(0)
+    landed(xr.at[pl.ds(1, NX - 1)], x_rs.at[0])
     for k in range(1, NX):
-        x_copy(k).wait_recv()
         plane = plane + xr[k].astype(F32)
     zs[...] = plane.reshape(NZ, 8, 128)
     for m in z_order:
@@ -384,12 +390,11 @@
     def t_copy(dy, dc):
         slot = core * NY + y
         seq = s if dc == 0 else sib
-        return send(tiles.at[slot], tiles.at[slot], t_ss.at[dy * 2 + dc], t_rs.at[slot], seq, at_y(dy))
+        return send(tiles.at[slot], tiles.at[slot], t_ss.at[0], t_rs.at[0], seq, at_y(dy))
 
     others = [(dy, dc) for dy in range(NY) for dc in range(2) if (dy, dc) != (0, 0)]
 
-    for m in z_order:
-        z_copy(m).wait_recv()
+    landed(zr.at[pl.ds(1, NZ - 1)], z_rs.at[0])
     tile = zs[z]
     for m in range(1, NZ):
         tile = tile + zr[m]
@@ -397,40 +402,27 @@
     for dy, dc in others:
         t_copy(dy, dc).start()
 
+    landed(er, e_rs.at[0])
     for h in heads:
-        for r in range(PARTS):
-            for t in far:
-                e_copy(t, h, r).wait_recv()
         dqo[:, cols(h)] = (dqa[h] + er[h, 0].astype(F32) + er[h, 1].astype(F32)).astype(BF16)
     query_out = pltpu.make_async_copy(dqo, dq_out.at[0], out_sem.at[3])
     query_out.start()
 
-    for dy, dc in others:
-        slot = (core if dc == 0 else 1 - core) * NY + at_y(dy)
-        send(tiles.at[slot], tiles.at[slot], t_ss.at[dy * 2 + dc], t_rs.at[slot], s, y).wait_recv()
+    for ref, sem in (
+        (ps, q_ss), (ps, m_ss), (dsend, d_ss), (es, e_ss), (gs, p_ss), (ya, ya_ss), (yb, yb_ss),
+        (xs.at[pl.ds(1, NX - 1)], x_ss), (zs.at[pl.ds(0, NZ - 1)], z_ss),
+    ):
+        sent(ref, sem.at[0])
+    for out in (gate_out, key_out, value_out, query_out):
+        out.wait()
+
+    arrived = tiles.at[pl.ds(0, 2 * NY - 1)]
+    landed(arrived, t_rs.at[0])
     lower = jnp.broadcast_to(core, (4, 128)) == 0
     for slot in range(2 * NY):
         full = tiles[slot]
         wg_out[:, slot * 128:(slot + 1) * 128] = jnp.where(lower, full[:4], full[4:])
-
-    for h in heads:
-        for t in far:
-            for r in range(PARTS):
-                for copy in (q_copy, m_copy, d_copy, e_copy):
-                    copy(t, h, r).wait_send()
-    for k in range(NX):
-        p_copy(k).wait_send()
-        for i in range(2):
-            ya_copy(k, i).wait_send()
-            yb_copy(k, i).wait_send()
-        if k:
-            x_copy(k).wait_send()
-    for m in z_order:
-        z_copy(m).wait_send()
-    for dy, dc in others:
-        t_copy(dy, dc).wait_send()
-    for out in (gate_out, key_out, value_out, query_out):
-        out.wait()
+    sent(arrived, t_ss.at[0])
 
 
 def finish(*refs):
@@ -457,6 +449,7 @@
 
 def local(queries, keys, values, gates, out_weight, out_grad, lengths, pattern):
     block = (HEADS, ROWS, HEAD_DIM)
+    block_t = (HEADS, HEAD_DIM, ROWS)
     two = (HEADS, BAND, ROWS, HEAD_DIM)
     three = (HEADS, BAND + 1, ROWS, HEAD_DIM)
     band = (BAND + 1, ROWS, ROWS)
@@ -465,25 +458,30 @@
     smem = pltpu.SMEM
     scratch = [
         smem(lengths.shape, jnp.int32), smem(pattern.shape, jnp.int32),
-        vmem(three, BF16), vmem(block, BF16), vmem(block, BF16), vmem(block, BF16),
-        vmem((2 * HEADS, ROWS, HEAD_DIM), BF16), vmem((WIDTH, MODEL), BF16),
+        vmem(three, BF16), vmem(rows, BF16), vmem(rows, BF16), vmem(rows, BF16),
+        vmem((ROWS, MODEL), BF16), vmem((WIDTH, MODEL), BF16),
+        vmem(block_t, BF16), vmem(block_t, BF16),
         vmem(band, F32), vmem(band, F32), vmem(block, F32), vmem(block, F32),
         vmem(two, BF16), vmem(two, BF16),
         vmem(three, BF16), vmem(two, BF16), vmem(two, BF16), vmem(two, BF16),
-        vmem((HEADS,) + band, BF16), vmem((HEADS,) + band, F32),
+        vmem((HEADS, ROWS, ROWS), BF16), vmem((HEADS, PARTS, ROWS, BAND * PART), BF16),
+        vmem(block_t, BF16), vmem((HEADS, PARTS, HEAD_DIM, BAND * PART), BF16),
+        vmem((HEADS, ROWS, ROWS), F32), vmem((HEADS, PARTS, BAND * PART, ROWS), F32),
         vmem((NZ, NX, 8, ROWS), F32),
         vmem((NX, NY, NZ * 8, 128), F32), vmem((NX, NY, NZ * 8, 128), BF16), vmem((NX, NY, NZ * 8, 128), BF16),
         vmem((NX, 2, NZ * 4, 128), BF16), vmem((NX, 2, NZ * 4, 128), BF16),
         vmem((NX, 2, NZ * 8, 128), BF16), vmem((NX, 2, NZ * 8, 128), BF16),
         vmem((NX, NZ * 8, 128), BF16), vmem((NX, NZ * 8, 128), BF16),
         vmem((NZ, 8, 128), F32), vmem((NZ, 8, 128), F32), vmem((2 * NY, 8, 128), F32),
-        vmem(block, F32), vmem(block, F32), vmem(block, F32),
+        vmem(block, F32), vmem(block_t, F32), vmem(block, F32),
         vmem(rows, BF16), vmem(rows, BF16), vmem(rows, BF16), vmem(rows, BF16),
     ]
     dma = pltpu.SemaphoreType.DMA
-    scratch += [dma((5, 2 * HEADS)), dma((3,)), dma((4,))]
-    scratch += [dma((BAND, HEADS, PARTS))] * 8
-    scratch += [dma((NX,))] * 2 + [dma((NX, 2))] * 4 + [dma((NX,))] * 2 + [dma((NZ,))] * 2 + [dma((2 * NY,))] * 2
+    one = dma((1,))
+    scratch += [dma((11,)), dma((4,))]
+    scratch += [one, dma((HEADS, PARTS)), one, dma((PARTS,)), one, dma((HEADS, PARTS)), one, one]
+    scratch += [one, dma((NX,)), one, dma((NX,)), one, dma((NX,))]
+    scratch += [one] * 6
     anywhere = pl.BlockSpec(memory_space=pl.ANY)
     grad = jax.ShapeDtypeStruct((1, ROWS, WIDTH), BF16)
     operands = (lengths, pattern, queries, keys, values, gates, out_weight, out_grad)

time: 62.4 us -> 60 us (0.962)
  Pallas kernels: 61.7 us -> 59.3 us
    pallas_call x1, Pallas kernels: 60.6 us -> 58.2 us  [local(): pl.pallas_call(kernel, out_shape=(grad, grad, grad, grad, jax.ShapeDtypeS...]
where the time goes in v2:
time: 60 us; the launch traced here: 59.9 us
  Pallas kernels  59.3 us (99%)
  between operations  0.64 us (1%)
    pallas_call x1, Pallas kernels, local(): pl.pallas_call(kernel, out_shape=(grad, grad, grad, grad, jax.ShapeDtypeS...  58.2 us

profile of v2, /device:TPU:1, one launch (start us, length us, event | category | flops | bytes accessed | tf_op | source)
XLA Modules:
  0.0 59.9 jit_solution(5008294660548828139)
XLA Ops:
  0.6 58.2 %shard_map.119 = (bf16[1,256,512]{2,1,0:T(8,128)(2,1)S(1)}, bf16[1,256,512]{2,1,0:T(8,128)(2,1)S(1)}, bf16[1,256,512]{2,1,0:T(8,128)(2,1)S(1)}, bf16[1,256,512]{2,1,0:T(8,128)(2,1)S(1)}, f32[4,1024]{1,0:T(4,128)S(1)}) custom-call(s32[1,4]{1,0:T(1,128)} %len_in.1, s32[1,1,2]{2,1,0:T(1,128)} %pat_in.1, bf16[1,256,512]{2,1,0:T(8,128)(2,1)} %q_in.1, ...), custom_call_target="tpu_custom_call" | custom-call | flops 2000000000 | bytes 5242880 | tf_op jit(solution)/shard_map/pallas_call | solution.py:488
  58.9 1.0 %shard_map.120 = (bf16[1,256,512]{2,1,0:T(8,128)(2,1)}, bf16[1,256,512]{2,1,0:T(8,128)(2,1)}, bf16[1,256,512]{2,1,0:T(8,128)(2,1)}, bf16[1,256,512]{2,1,0:T(8,128)(2,1)}, f32[4,1024]{1,0:T(4,128)}) custom-call(bf16[1,256,512]{2,1,0:T(8,128)(2,1)S(1)} %get-tuple-element.10.refs_0_, bf16[1,256,512]{2,1,0:T(8,128)(2,1)S(1)} %get-tuple-element.11.refs_1_, ...), custom_call_target="tpu_custom_call" | custom-call | tf_op jit(solution)/shard_map/pallas_call | solution.py:440

commit v3 on v2

--- a/solution.py
+++ b/solution.py
@@ -45,12 +45,12 @@
 def kernel(
     len_in, pat_in, q_in, k_in, v_in, gate_in, w_in, og_in,
     dq_out, dk_out, dv_out, dg_out, wg_out,
-    len_ref, pat_ref, q3, kb, vb, gb, ogb, wb, kt, vt, mask, half, dgt, mix,
-    ps, mr, d3, dsend, es, er, attn_own, attn_far, qt_own, qt_far, slope_own, slope_far, gt,
-    gown, gs, gr, ya, yar, yb, ybr, xs, xr, zs, zr, tiles,
+    len_ref, pat_ref, q3, kb, vb, gb, ogb, ogs, wb, kt, vt, mask, half, dgt, mix,
+    ps, mr, d3, dsend, es, er, attn_own, attn_far, qt_own, qt_far, slope_own, slope_far, gt, gtb, gtr,
+    gown, ya, yar, yb, ybr, xs, xr, zs, zr, tiles,
     dqa, dka, dva, dqo, dko, dvo, dgo,
     ld_sem, out_sem, q_ss, q_rs, m_ss, m_rs, d_ss, d_rs, e_ss, e_rs,
-    p_ss, p_rs, ya_ss, ya_rs, yb_ss, yb_rs, x_ss, x_rs, z_ss, z_rs, t_ss, t_rs,
+    o_ss, o_rs, g_ss, g_rs, ya_ss, ya_rs, yb_ss, yb_rs, x_ss, x_rs, z_ss, z_rs, t_ss, t_rs,
 ):
     s = lax.axis_index("seq")
     y = lax.axis_index("dp")
@@ -100,10 +100,10 @@
     k_load = pltpu.make_async_copy(k_in.at[0], kb, ld_sem.at[4])
     v_load = pltpu.make_async_copy(v_in.at[0], vb, ld_sem.at[5])
     gate_load = pltpu.make_async_copy(gate_in.at[0], gb, ld_sem.at[6])
-    og_load = pltpu.make_async_copy(og_in.at[0], ogb, ld_sem.at[7])
+    og_loads = [pltpu.make_async_copy(og_in.at[0, :, c * WIDTH:(c + 1) * WIDTH], ogb.at[c], ld_sem.at[11 + c]) for c in range(2)]
     w_load = pltpu.make_async_copy(w_in, wb, ld_sem.at[8])
     few_loads = [pltpu.make_async_copy(len_in, len_ref, ld_sem.at[9]), pltpu.make_async_copy(pat_in, pat_ref, ld_sem.at[10])]
-    for load in [k_load, v_load] + few_loads + [og_load, w_load, gate_load]:
+    for load in [k_load, v_load] + few_loads + og_loads + [w_load, gate_load]:
         load.start()
 
     def send(src, dst, ss, rs, seq, dp):
@@ -195,9 +195,12 @@
         attn_own[h] = a.T
         qt_own[h] = q.T
 
-    og_load.wait()
+    for load in og_loads:
+        load.wait()
+    swap = send(ogb.at[1 - core], ogs, o_ss.at[0], o_rs.at[0], sib, y)
+    swap.start()
     w_load.wait()
-    og = ogb[...]
+    og = jnp.concatenate([ogb[0], ogb[1]], axis=1)
     for i in range(2):
         part = dot_nt(og, wb[pl.ds(i * 256, 256), :])
         dgt[2 * i] = part[:, :HEAD_DIM]
@@ -249,11 +252,22 @@
     def norm_part(r):
         landed(mr.at[:, :, rows_of(r)], m_rs.at[r])
         gated = [norm(pl.ds(r * PART + i * step_rows, step_rows)) for i in range(PART // step_rows)]
+        gtb[r] = jnp.concatenate(gated, axis=0).T
+        g_copy(r).start()
         for h in heads:
             for t in far:
                 d_copy(t, h, r).start()
-        gated = jnp.concatenate(gated, axis=0)
-        gt[:, :, :, rows_of(r)] = gated.T.astype(F32).reshape(NZ, NX, 8, PART)
+        spread(gtb, r, r)
+
+    def g_copy(r):
+        return send(gtb.at[r], gtr.at[r], g_ss.at[0], g_rs.at[r], sib, y)
+
+    def spread(part, r, at):
+        gt[:, :, :, at * PART:(at + 1) * PART] = part[r].astype(F32).reshape(NZ, NX, 8, PART)
+
+    def other_part(r):
+        landed(gtr.at[r], g_rs.at[r])
+        spread(gtr, r, PARTS + r)
 
     def backward(d, slope, h, q_t, attn_t):
         ds = (dot(d, vt[h]) * slope).astype(BF16)
@@ -288,6 +302,8 @@
     far_forward(2, 1)
     far_forward(3, 1)
     own_backward(0)
+    landed(ogs, o_rs.at[0])
+    other_part(0)
     norm_part(1)
 
     piece = NZ * 8
@@ -298,9 +314,6 @@
     down = at_y(NY - 1)
     across = at_y(2)
 
-    def p_copy(k):
-        return send(gs.at[k], gr.at[k], p_ss.at[0], p_rs.at[k], sib, y)
-
     def ya_copy(k, i):
         return send(ya.at[k, i], yar.at[k, i], ya_ss.at[0], ya_rs.at[k], s, (up, down)[i])
 
@@ -311,22 +324,23 @@
         return send(xs.at[k], xr.at[k], x_ss.at[0], x_rs.at[0], at_x(k), y)
 
     order = (2, 1, 3, 0)
-    other = ogb[:, pl.ds(pl.multiple_of((1 - core) * WIDTH, WIDTH), WIDTH)]
+    near_rows = (2 * PARTS - 1) * PART
+
+    def product(k, events, grad):
+        return dot(gt[:, x_of(k), :, events].reshape(piece, -1).astype(BF16), grad)
+
+    mine = jnp.concatenate([ogb[core], ogs[:ROWS - PART]], axis=0)
     for k in order:
-        part = dot(gt[:, x_of(k)].reshape(piece, ROWS).astype(BF16), other)
-        for i in range(NY):
-            gs[k, i] = part[:, cols(i)].astype(BF16)
-        p_copy(k).start()
-    mine = ogb[:, pl.ds(pl.multiple_of(core * WIDTH, WIDTH), WIDTH)]
-    for k in order:
-        part = dot(gt[:, x_of(k)].reshape(piece, ROWS).astype(BF16), mine)
+        part = product(k, slice(0, near_rows), mine)
         for i in range(NY):
             gown[k, i] = part[:, cols(i)]
+    far_backward(0, 0)
+    other_part(PARTS - 1)
 
     for k in order:
-        p_copy(k).wait_recv()
+        part = product(k, slice(near_rows, 2 * ROWS), ogs[ROWS - PART:])
         for i in range(NY):
-            gown[k, i] = gown[k, i] + gr[k, i].astype(F32)
+            gown[k, i] = gown[k, i] + part[:, cols(i)]
         ya[k, 0] = gown[k, across, low].astype(BF16)
         ya[k, 1] = gown[k, across, high].astype(BF16)
         for i in range(2):
@@ -352,20 +366,16 @@
         xs[k] = y_sum(k).astype(BF16)
         x_copy(k).start()
 
-    far_backward(0, 0)
     far_backward(1, 0)
-    y_pass(2)
-    y_pass(1)
     far_backward(2, 0)
-    y_pass(3)
-    y_pass(0)
     far_backward(3, 0)
+    for k in order:
+        y_pass(k)
     own_backward(1)
-    x_start(2)
     far_backward(0, 1)
-    x_start(1)
     far_backward(1, 1)
-    x_start(3)
+    for k in order[:-1]:
+        x_start(k)
 
     z_order = (8, 7, 9, 6, 10, 5, 11, 4, 12, 3, 13, 2, 14, 1, 15)
 
@@ -409,7 +419,7 @@
     query_out.start()
 
     for ref, sem in (
-        (ps, q_ss), (ps, m_ss), (dsend, d_ss), (es, e_ss), (gs, p_ss), (ya, ya_ss), (yb, yb_ss),
+        (ps, q_ss), (ps, m_ss), (dsend, d_ss), (es, e_ss), (ogs, o_ss), (gtb, g_ss), (ya, ya_ss), (yb, yb_ss),
         (xs.at[pl.ds(1, NX - 1)], x_ss), (zs.at[pl.ds(0, NZ - 1)], z_ss),
     ):
         sent(ref, sem.at[0])
@@ -459,7 +469,7 @@
     scratch = [
         smem(lengths.shape, jnp.int32), smem(pattern.shape, jnp.int32),
         vmem(three, BF16), vmem(rows, BF16), vmem(rows, BF16), vmem(rows, BF16),
-        vmem((ROWS, MODEL), BF16), vmem((WIDTH, MODEL), BF16),
+        vmem((2,) + rows, BF16), vmem(rows, BF16), vmem((WIDTH, MODEL), BF16),
         vmem(block_t, BF16), vmem(block_t, BF16),
         vmem(band, F32), vmem(band, F32), vmem(block, F32), vmem(block, F32),
         vmem(two, BF16), vmem(two, BF16),
@@ -467,8 +477,8 @@
         vmem((HEADS, ROWS, ROWS), BF16), vmem((HEADS, PARTS, ROWS, BAND * PART), BF16),
         vmem(block_t, BF16), vmem((HEADS, PARTS, HEAD_DIM, BAND * PART), BF16),
         vmem((HEADS, ROWS, ROWS), F32), vmem((HEADS, PARTS, BAND * PART, ROWS), F32),
-        vmem((NZ, NX, 8, ROWS), F32),
-        vmem((NX, NY, NZ * 8, 128), F32), vmem((NX, NY, NZ * 8, 128), BF16), vmem((NX, NY, NZ * 8, 128), BF16),
+        vmem((NZ, NX, 8, 2 * ROWS), F32), vmem((PARTS, WIDTH, PART), BF16), vmem((PARTS, WIDTH, PART), BF16),
+        vmem((NX, NY, NZ * 8, 128), F32),
         vmem((NX, 2, NZ * 4, 128), BF16), vmem((NX, 2, NZ * 4, 128), BF16),
         vmem((NX, 2, NZ * 8, 128), BF16), vmem((NX, 2, NZ * 8, 128), BF16),
         vmem((NX, NZ * 8, 128), BF16), vmem((NX, NZ * 8, 128), BF16),
@@ -478,9 +488,9 @@
     ]
     dma = pltpu.SemaphoreType.DMA
     one = dma((1,))
-    scratch += [dma((11,)), dma((4,))]
+    scratch += [dma((13,)), dma((4,))]
     scratch += [one, dma((HEADS, PARTS)), one, dma((PARTS,)), one, dma((HEADS, PARTS)), one, one]
-    scratch += [one, dma((NX,)), one, dma((NX,)), one, dma((NX,))]
+    scratch += [one, one, one, dma((PARTS,)), one, dma((NX,)), one, dma((NX,))]
     scratch += [one] * 6
     anywhere = pl.BlockSpec(memory_space=pl.ANY)
     grad = jax.ShapeDtypeStruct((1, ROWS, WIDTH), BF16)

time: 60 us -> 59.5 us (level)
  no operation moved by 1% of the time
where the time goes in v3:
time: 59.5 us; the launch traced here: 59.4 us
  Pallas kernels  58.7 us (99%)
  between operations  0.64 us (1%)
    pallas_call x1, Pallas kernels, local(): pl.pallas_call(kernel, out_shape=(grad, grad, grad, grad, jax.ShapeDtypeS...  57.7 us

profile of v3, /device:TPU:1, one launch (start us, length us, event | category | flops | bytes accessed | tf_op | source)
XLA Modules:
  0.0 59.4 jit_solution(18060873628117529564)
XLA Ops:
  0.6 57.7 %shard_map.119 = (bf16[1,256,512]{2,1,0:T(8,128)(2,1)S(1)}, bf16[1,256,512]{2,1,0:T(8,128)(2,1)S(1)}, bf16[1,256,512]{2,1,0:T(8,128)(2,1)S(1)}, bf16[1,256,512]{2,1,0:T(8,128)(2,1)S(1)}, f32[4,1024]{1,0:T(4,128)S(1)}) custom-call(s32[1,4]{1,0:T(1,128)} %len_in.1, s32[1,1,2]{2,1,0:T(1,128)} %pat_in.1, bf16[1,256,512]{2,1,0:T(8,128)(2,1)} %q_in.1, ...), custom_call_target="tpu_custom_call" | custom-call | flops 2000000000 | bytes 5242880 | tf_op jit(solution)/shard_map/pallas_call | solution.py:498
  58.3 1.0 %shard_map.120 = (bf16[1,256,512]{2,1,0:T(8,128)(2,1)}, bf16[1,256,512]{2,1,0:T(8,128)(2,1)}, bf16[1,256,512]{2,1,0:T(8,128)(2,1)}, bf16[1,256,512]{2,1,0:T(8,128)(2,1)}, f32[4,1024]{1,0:T(4,128)}) custom-call(bf16[1,256,512]{2,1,0:T(8,128)(2,1)S(1)} %get-tuple-element.10.refs_0_, bf16[1,256,512]{2,1,0:T(8,128)(2,1)S(1)} %get-tuple-element.11.refs_1_, ...), custom_call_target="tpu_custom_call" | custom-call | tf_op jit(solution)/shard_map/pallas_call | solution.py:450

commit v4 on v3

--- a/solution.py
+++ b/solution.py
@@ -190,8 +190,10 @@
     v_load.wait()
     for h in heads:
         vt[h] = vb[:, cols(h)].T
-    for h in heads:
-        q, a, slope_own[h], mix[h] = forward(own, pl.ds(0, ROWS), h)
+    made = [forward(own, pl.ds(0, ROWS), h) for h in heads]
+    for h, (q, a, slope, part) in zip(heads, made):
+        slope_own[h] = slope
+        mix[h] = part
         attn_own[h] = a.T
         qt_own[h] = q.T
 
@@ -207,14 +209,19 @@
         dgt[2 * i + 1] = part[:, HEAD_DIM:]
     gate_load.wait()
 
-    def far_forward(h, r):
-        landed(q3.at[h, both, rows_of(r)], q_rs.at[h, r])
-        q, a, slope_far[h, r], part = forward(both, rows_of(r), h)
-        ps[h, :, rows_of(r)] = part.astype(BF16).reshape(BAND, PART, HEAD_DIM)
-        for t in far:
-            m_copy(t, h, r).start()
-        attn_far[h, r] = a.T
-        qt_far[h, r] = q.T
+    def far_forward(group, r):
+        for h in group:
+            landed(q3.at[h, both, rows_of(r)], q_rs.at[h, r])
+        made = [forward(both, rows_of(r), h) for h in group]
+        for h, (_, _, slope, part) in zip(group, made):
+            ps[h, :, rows_of(r)] = part.astype(BF16).reshape(BAND, PART, HEAD_DIM)
+            slope_far[h, r] = slope
+        for h in group:
+            for t in far:
+                m_copy(t, h, r).start()
+        for h, (q, a, _, _) in zip(group, made):
+            attn_far[h, r] = a.T
+            qt_far[h, r] = q.T
 
     near = [jnp.where(pat_ref[0, 0, t] > 0, 1.0, 0.0).astype(F32) for t in range(BAND)]
 
@@ -275,32 +282,39 @@
 
     def own_backward(r):
         lanes = slice(r * PART, (r + 1) * PART)
-        for h in heads:
-            dq, dk, dv = backward(d3[h, 0, rows_of(r)], slope_own[h, rows_of(r)], h, qt_own[h, :, lanes], attn_own[h, :, lanes])
+        made = [
+            backward(d3[h, 0, rows_of(r)], slope_own[h, rows_of(r)], h, qt_own[h, :, lanes], attn_own[h, :, lanes]) for h in heads
+        ]
+        for h, (dq, dk, dv) in zip(heads, made):
             dqa[h, rows_of(r)] = dq
             dka[h] = dk if r == 0 else dka[h] + dk
             dva[h] = dv if r == 0 else dva[h] + dv
 
-    def far_backward(h, r):
-        landed(d3.at[h, both, rows_of(r)], d_rs.at[h, r])
-        dq, dk, dv = backward(flat(d3[h, both, rows_of(r)]), slope_far[h, r], h, qt_far[h, r], attn_far[h, r])
-        es[h, :, rows_of(r)] = dq.astype(BF16).reshape(BAND, PART, HEAD_DIM)
-        for t in far:
-            e_copy(t, h, r).start()
-        if r < PARTS - 1:
-            dka[h] = dka[h] + dk
-            dva[h] = dva[h] + dv
-        else:
-            dko[:, cols(h)] = (dka[h] + dk).T.astype(BF16)
-            dvo[:, cols(h)] = (dva[h] + dv).astype(BF16)
-
-    for h in heads:
-        far_forward(h, 0)
-    far_forward(0, 1)
-    far_forward(1, 1)
+    def far_backward(group, r):
+        for h in group:
+            landed(d3.at[h, both, rows_of(r)], d_rs.at[h, r])
+        made = [
+            backward(flat(d3[h, both, rows_of(r)]), slope_far[h, r], h, qt_far[h, r], attn_far[h, r]) for h in group
+        ]
+        for h, (dq, dk, dv) in zip(group, made):
+            es[h, :, rows_of(r)] = dq.astype(BF16).reshape(BAND, PART, HEAD_DIM)
+            if r < PARTS - 1:
+                dka[h] = dka[h] + dk
+                dva[h] = dva[h] + dv
+            else:
+                dko[:, cols(h)] = (dka[h] + dk).T.astype(BF16)
+                dvo[:, cols(h)] = (dva[h] + dv).astype(BF16)
+        for h in group:
+            for t in far:
+                e_copy(t, h, r).start()
+
+    first, last = (0, 1), (2, 3)
+    far_forward(first, 0)
+    far_forward(last, 0)
+    far_forward(first, 1)
     norm_part(0)
-    far_forward(2, 1)
-    far_forward(3, 1)
+    far_forward((2,), 1)
+    far_forward((3,), 1)
     own_backward(0)
     landed(ogs, o_rs.at[0])
     other_part(0)
@@ -334,7 +348,7 @@
         part = product(k, slice(0, near_rows), mine)
         for i in range(NY):
             gown[k, i] = part[:, cols(i)]
-    far_backward(0, 0)
+    far_backward(first, 0)
     other_part(PARTS - 1)
 
     for k in order:
@@ -366,14 +380,11 @@
         xs[k] = y_sum(k).astype(BF16)
         x_copy(k).start()
 
-    far_backward(1, 0)
-    far_backward(2, 0)
-    far_backward(3, 0)
+    far_backward(last, 0)
     for k in order:
         y_pass(k)
     own_backward(1)
-    far_backward(0, 1)
-    far_backward(1, 1)
+    far_backward(first, 1)
     for k in order[:-1]:
         x_start(k)
 
@@ -390,8 +401,7 @@
     for m in z_order:
         z_copy(m).start()
 
-    far_backward(2, 1)
-    far_backward(3, 1)
+    far_backward(last, 1)
     key_out = pltpu.make_async_copy(dko, dk_out.at[0], out_sem.at[1])
     value_out = pltpu.make_async_copy(dvo, dv_out.at[0], out_sem.at[2])
     key_out.start()

time: 59.5 us -> 61.9 us (1.040)
  Pallas kernels: 58.7 us -> 61.2 us
    pallas_call x1, Pallas kernels: 57.7 us -> 60.1 us  [local(): pl.pallas_call(kernel, out_shape=(grad, grad, grad, grad, jax.ShapeDtypeS...]
where the time goes in v4:
time: 61.9 us; the launch traced here: 61.8 us
  Pallas kernels  61.2 us (99%)
  between operations  0.64 us (1%)
    pallas_call x1, Pallas kernels, local(): pl.pallas_call(kernel, out_shape=(grad, grad, grad, grad, jax.ShapeDtypeS...  60.1 us

profile of v4, /device:TPU:1, one launch (start us, length us, event | category | flops | bytes accessed | tf_op | source)
XLA Modules:
  0.0 61.8 jit_solution(15511781315544069942)
XLA Ops:
  0.6 60.1 %shard_map.119 = (bf16[1,256,512]{2,1,0:T(8,128)(2,1)S(1)}, bf16[1,256,512]{2,1,0:T(8,128)(2,1)S(1)}, bf16[1,256,512]{2,1,0:T(8,128)(2,1)S(1)}, bf16[1,256,512]{2,1,0:T(8,128)(2,1)S(1)}, f32[4,1024]{1,0:T(4,128)S(1)}) custom-call(s32[1,4]{1,0:T(1,128)} %len_in.1, s32[1,1,2]{2,1,0:T(1,128)} %pat_in.1, bf16[1,256,512]{2,1,0:T(8,128)(2,1)} %q_in.1, ...), custom_call_target="tpu_custom_call" | custom-call | flops 2000000000 | bytes 5242880 | tf_op jit(solution)/shard_map/pallas_call | solution.py:508
  60.8 1.0 %shard_map.120 = (bf16[1,256,512]{2,1,0:T(8,128)(2,1)}, bf16[1,256,512]{2,1,0:T(8,128)(2,1)}, bf16[1,256,512]{2,1,0:T(8,128)(2,1)}, bf16[1,256,512]{2,1,0:T(8,128)(2,1)}, f32[4,1024]{1,0:T(4,128)}) custom-call(bf16[1,256,512]{2,1,0:T(8,128)(2,1)S(1)} %get-tuple-element.10.refs_0_, bf16[1,256,512]{2,1,0:T(8,128)(2,1)S(1)} %get-tuple-element.11.refs_1_, ...), custom_call_target="tpu_custom_call" | custom-call | tf_op jit(solution)/shard_map/pallas_call | solution.py:460

commit v5 on v3

--- a/solution.py
+++ b/solution.py
@@ -190,22 +190,23 @@
     v_load.wait()
     for h in heads:
         vt[h] = vb[:, cols(h)].T
-    for h in heads:
+    def own_forward(h):
         q, a, slope_own[h], mix[h] = forward(own, pl.ds(0, ROWS), h)
         attn_own[h] = a.T
         qt_own[h] = q.T
 
+    def up_rows(i):
+        og = jnp.concatenate([ogb[0], ogb[1]], axis=1)
+        part = dot_nt(og, wb[pl.ds(i * 256, 256), :])
+        dgt[2 * i] = part[:, :HEAD_DIM]
+        dgt[2 * i + 1] = part[:, HEAD_DIM:]
+
+    own_forward(0)
     for load in og_loads:
         load.wait()
     swap = send(ogb.at[1 - core], ogs, o_ss.at[0], o_rs.at[0], sib, y)
     swap.start()
-    w_load.wait()
-    og = jnp.concatenate([ogb[0], ogb[1]], axis=1)
-    for i in range(2):
-        part = dot_nt(og, wb[pl.ds(i * 256, 256), :])
-        dgt[2 * i] = part[:, :HEAD_DIM]
-        dgt[2 * i + 1] = part[:, HEAD_DIM:]
-    gate_load.wait()
+    own_forward(1)
 
     def far_forward(h, r):
         landed(q3.at[h, both, rows_of(r)], q_rs.at[h, r])
@@ -294,9 +295,17 @@
             dko[:, cols(h)] = (dka[h] + dk).T.astype(BF16)
             dvo[:, cols(h)] = (dva[h] + dv).astype(BF16)
 
-    for h in heads:
-        far_forward(h, 0)
+    far_forward(0, 0)
+    own_forward(2)
+    far_forward(1, 0)
+    own_forward(3)
+    far_forward(2, 0)
+    w_load.wait()
+    up_rows(0)
+    far_forward(3, 0)
+    up_rows(1)
     far_forward(0, 1)
+    gate_load.wait()
     far_forward(1, 1)
     norm_part(0)
     far_forward(2, 1)

time: 59.5 us -> 59.4 us (level)
  no operation moved by 1% of the time
where the time goes in v5:
time: 59.4 us; the launch traced here: 59.2 us
  Pallas kernels  58.6 us (99%)
  between operations  0.64 us (1%)
    pallas_call x1, Pallas kernels, local(): pl.pallas_call(kernel, out_shape=(grad, grad, grad, grad, jax.ShapeDtypeS...  57.6 us

profile of v5, /device:TPU:1, one launch (start us, length us, event | category | flops | bytes accessed | tf_op | source)
XLA Modules:
  0.0 59.2 jit_solution(7713675719671567859)
XLA Ops:
  0.6 57.6 %shard_map.119 = (bf16[1,256,512]{2,1,0:T(8,128)(2,1)S(1)}, bf16[1,256,512]{2,1,0:T(8,128)(2,1)S(1)}, bf16[1,256,512]{2,1,0:T(8,128)(2,1)S(1)}, bf16[1,256,512]{2,1,0:T(8,128)(2,1)S(1)}, f32[4,1024]{1,0:T(4,128)S(1)}) custom-call(s32[1,4]{1,0:T(1,128)} %len_in.1, s32[1,1,2]{2,1,0:T(1,128)} %pat_in.1, bf16[1,256,512]{2,1,0:T(8,128)(2,1)} %q_in.1, ...), custom_call_target="tpu_custom_call" | custom-call | flops 2000000000 | bytes 5242880 | tf_op jit(solution)/shard_map/pallas_call | solution.py:507
  58.2 1.0 %shard_map.120 = (bf16[1,256,512]{2,1,0:T(8,128)(2,1)}, bf16[1,256,512]{2,1,0:T(8,128)(2,1)}, bf16[1,256,512]{2,1,0:T(8,128)(2,1)}, bf16[1,256,512]{2,1,0:T(8,128)(2,1)}, f32[4,1024]{1,0:T(4,128)}) custom-call(bf16[1,256,512]{2,1,0:T(8,128)(2,1)S(1)} %get-tuple-element.10.refs_0_, bf16[1,256,512]{2,1,0:T(8,128)(2,1)S(1)} %get-tuple-element.11.refs_1_, ...), custom_call_target="tpu_custom_call" | custom-call | tf_op jit(solution)/shard_map/pallas_call | solution.py:459
